TPU v7x, 32 devices: a whole 2x2x4 slice. The times are simulated.
32 devices in a mesh: group: 4 (over y, core), dev: 8 (over z, x).
Axes of the slice: x: 2, y: 2, z: 4, core: 2. Of those that a mesh axis runs over, the one named last changes fastest.
Arguments:
- points: float32 [440, 16384], P(None, ('group', 'dev')), may hold values from -6 to 6
- residual: float32 [147, 16384], P(None, ('group', 'dev')), may hold values from -6 to 6
- coeffs: float32 [147, 16384], P(None, ('group', 'dev')), may hold values from -3 to 3
- owners: int32 [2], replicated, may hold values from 0 to 31
- offsets: int32 [2], replicated, may hold values from 0 to 256
Outputs:
- new_residual: float32 [147, 16384], P(None, ('group', 'dev'))
- new_coeffs: float32 [147, 16384], P(None, ('group', 'dev'))
All inputs are finite; a program needn't handle non-finite values.
Results may differ from a plain program's by a relative error of at most 0.0003.
Values sent between devices are 32-bit elements; how exact they have to be, the bound alone decides.
A program may use at most 64 MiB of HBM per device.

v0:
```python
import functools

import jax
import jax.numpy as jnp
from jax import lax
from jax.experimental import pallas as pl
from jax.experimental.pallas import tpu as pltpu
from jax.sharding import PartitionSpec as P

BLOCK = 256
LANES = 128
SUB = 8

ridge = 2.0
step_norm = 1.5

MESH = pl.DeviceIdType.MESH
F32 = jnp.float32


def exact_dot(a, b, dims):
    return lax.dot_general(
        a, b, (dims, ((), ())), precision=lax.Precision.HIGHEST, preferred_element_type=F32
    )


NN = ((1,), (0,))
NT = ((1,), (1,))


def low_dot(a, b):
    return jnp.dot(a.astype(jnp.bfloat16), b.astype(jnp.bfloat16), preferred_element_type=F32)


def split_dot(a, b, dims=NN):
    ah, bh = a.astype(jnp.bfloat16), b.astype(jnp.bfloat16)
    al = (a - ah.astype(F32)).astype(jnp.bfloat16)
    bl = (b - bh.astype(F32)).astype(jnp.bfloat16)
    dot = lambda u, v: lax.dot_general(u, v, (dims, ((), ())), preferred_element_type=F32)
    return dot(ah, bh) + (dot(ah, bl) + dot(al, bh))


def split_three(x):
    high = x.astype(jnp.bfloat16)
    rest = x - high.astype(F32)
    mid = rest.astype(jnp.bfloat16)
    return high, mid, (rest - mid.astype(F32)).astype(jnp.bfloat16)


def line_width(n_dev):
    width = 1
    while n_dev % (2 * width) == 0 and 4 * width * width <= n_dev:
        width *= 2
    return width


class Layout:
    def __init__(self, n_group, n_dev):
        self.n_dev = n_dev
        self.width = line_width(n_dev)
        self.plane = n_group * self.width
        self.line = n_dev // self.width
        self.cores = 2 if n_group % 2 == 0 else 1
        self.chips = self.plane // self.cores

    def share(self, tiles):
        return -(-tiles // self.plane)


class Sum:
    def __init__(self, layout, at, share, refs):
        self.layout, self.share = layout, share
        self.group, self.dev = at
        self.terms, self.landed, self.held, self.crossed, self.total, self.sems = refs
        self.place = self.group * layout.width + lax.rem(self.dev, layout.width)
        self.plane = self.dev // layout.width
        self.started = []

    def peer_in_plane(self, k):
        to = lax.rem(self.place + k, self.layout.plane)
        width = self.layout.width
        return to, (to // width, self.plane * width + lax.rem(to, width))

    def peer_in_line(self, k):
        to = lax.rem(self.plane + k, self.layout.line)
        width = self.layout.width
        return self.group, to * width + lax.rem(self.dev, width)

    def piece(self, index):
        return pl.ds(index * self.share, self.share)

    def send(self, src, dst, sem, to):
        copy = pltpu.make_async_remote_copy(
            src_ref=src,
            dst_ref=dst,
            send_sem=self.sems.at[0, sem],
            recv_sem=self.sems.at[1, sem],
            device_id=to,
            device_id_type=MESH,
        )
        copy.start()
        self.waiting.append(copy)

    def arrive(self):
        for copy in self.waiting:
            copy.wait_recv()
        self.started += self.waiting

    def scatter(self):
        self.waiting = []
        for k in range(1, self.layout.plane):
            to, device = self.peer_in_plane(k)
            self.send(self.terms.at[self.piece(to)], self.landed.at[self.piece(k - 1)], k - 1, device)

    def cross(self):
        self.arrive()
        total = self.terms[self.piece(self.place)]
        for k in range(self.layout.plane - 1):
            total = total + self.landed[self.piece(k)]
        self.held[...] = total
        self.waiting = []
        first = self.layout.plane - 1
        for k in range(1, self.layout.line):
            self.send(self.held, self.crossed.at[self.piece(k - 1)], first + k - 1, self.peer_in_line(k))

    def gather(self):
        self.arrive()
        total = self.held[...]
        for k in range(self.layout.line - 1):
            total = total + self.crossed[self.piece(k)]
        mine = self.total.at[self.piece(self.place)]
        mine[...] = total
        self.waiting = []
        first = self.layout.plane + self.layout.line - 2
        for k in range(1, self.layout.plane):
            self.send(mine, mine, first + k - 1, self.peer_in_plane(k)[1])

    def relay(self):
        pass

    def forward(self):
        pass

    def finish(self):
        self.arrive()

    def settle(self):
        for copy in self.started:
            copy.wait_send()


class PairedSum(Sum):
    def __init__(self, *args):
        super().__init__(*args)
        layout = self.layout
        self.core = lax.rem(self.group, layout.cores)
        self.chip = (self.group // layout.cores) * layout.width + lax.rem(self.dev, layout.width)
        self.place = self.core * layout.chips + self.chip

    def sibling(self):
        return self.group + 1 - 2 * self.core, self.dev

    def other_chip(self, k):
        layout = self.layout
        to = lax.rem(self.chip + k, layout.chips)
        group = (to // layout.width) * layout.cores + self.core
        return to, (group, self.plane * layout.width + lax.rem(to, layout.width))

    def scatter(self):
        layout = self.layout
        self.waiting = []
        for k in range(1, layout.chips + 1):
            to = (1 - self.core) * layout.chips + lax.rem(self.chip + k, layout.chips)
            self.send(self.terms.at[self.piece(to)], self.landed.at[self.piece(k - 1)], k - 1, self.sibling())

    def relay(self):
        layout = self.layout
        pairs, self.waiting = self.waiting, []
        for k in range(1, layout.chips + 1):
            pairs[k - 1].wait_recv()
            to, device = self.other_chip(k)
            mine = self.piece(self.core * layout.chips + to)
            self.terms[mine] = self.terms[mine] + self.landed[self.piece(k - 1)]
            if k < layout.chips:
                slot = layout.chips + k - 1
                self.send(self.terms.at[mine], self.landed.at[self.piece(slot)], slot, device)
        self.started += pairs

    def cross(self):
        layout = self.layout
        self.arrive()
        total = self.terms[self.piece(self.place)]
        for k in range(1, layout.chips):
            total = total + self.landed[self.piece(layout.chips + k - 1)]
        self.held[...] = total
        self.waiting = []
        first = layout.plane - 1
        for k in range(1, layout.line):
            self.send(self.held, self.crossed.at[self.piece(k - 1)], first + k - 1, self.peer_in_line(k))

    def gather(self):
        layout = self.layout
        self.arrive()
        total = self.held[...]
        for k in range(layout.line - 1):
            total = total + self.crossed[self.piece(k)]
        mine = self.total.at[self.piece(self.place)]
        mine[...] = total
        self.waiting = []
        first = layout.plane + layout.line - 2
        for k in range(1, layout.chips):
            self.send(mine, mine, first + k - 1, self.other_chip(k)[1])
        chips, self.waiting = self.waiting, []
        self.send(mine, mine, first + layout.chips - 1, self.sibling())
        self.chip_copies = chips

    def forward(self):
        layout = self.layout
        first = layout.plane + layout.line - 2 + layout.chips - 1
        for k in range(1, layout.chips):
            self.chip_copies[k - 1].wait_recv()
            source = lax.rem(self.chip + layout.chips - k, layout.chips)
            where = self.total.at[self.piece(self.core * layout.chips + source)]
            self.send(where, where, first + k, self.sibling())
        self.started += self.chip_copies


def sum_scratch(layout, share):
    tile = (SUB, LANES)
    copies = 2 * layout.plane + layout.line - 1
    return [
        pltpu.VMEM((layout.plane * share,) + tile, F32),
        pltpu.VMEM((max(layout.plane - 1, 1) * share,) + tile, F32),
        pltpu.VMEM((share,) + tile, F32),
        pltpu.VMEM((max(layout.line - 1, 1) * share,) + tile, F32),
        pltpu.VMEM((layout.plane * share,) + tile, F32),
        pltpu.SemaphoreType.DMA((2, copies)),
    ]


def to_tiles(ref, value):
    rows, columns = value.shape
    half = rows // SUB
    for c in range(columns // LANES):
        ref[c * half : (c + 1) * half] = value[:, c * LANES : (c + 1) * LANES].reshape(half, SUB, LANES)
    left = ref.shape[0] - half * (columns // LANES)
    if left:
        ref[ref.shape[0] - left :] = jnp.zeros((left, SUB, LANES), F32)


def from_tiles(ref, rows, columns):
    half = rows // SUB
    return jnp.concatenate(
        [ref[c * half : (c + 1) * half].reshape(rows, LANES) for c in range(columns // LANES)], axis=1
    )


def kernel(layout, n_group, owners_in, offsets_in, points_in, residual_in, change, *scratch):
    owners, offsets, points, residual, padded, flipped, tiles, loads = scratch[:8]
    sums = [scratch[8 + 6 * i : 14 + 6 * i] for i in range(4)]
    group, dev = lax.axis_index("group"), lax.axis_index("dev")
    me = group * layout.n_dev + dev
    features, here_points = points.shape
    classes = residual.shape[0]
    rows = padded.shape[0]

    copies = [
        pltpu.make_async_copy(src, dst, loads.at[i])
        for i, (src, dst) in enumerate(
            [(points_in, points), (owners_in, owners), (offsets_in, offsets), (residual_in, residual)]
        )
    ]
    for copy in copies:
        copy.start()

    blocks_share = sums[0][2].shape[0]
    grads_share = sums[2][2].shape[0]
    BlockSum = PairedSum if layout.cores == 2 else Sum
    spread = [BlockSum(layout, (group, dev), blocks_share, sums[i]) for i in range(2)]
    grads = [Sum(layout, (group, dev), grads_share, sums[2 + i]) for i in range(2)]

    barrier = pltpu.get_barrier_semaphore()
    peers = [grads[0].peer_in_plane(k)[1] for k in range(1, layout.plane)]
    peers += [grads[0].peer_in_line(k) for k in range(1, layout.line)]
    for peer in peers:
        pl.semaphore_signal(barrier, inc=1, device_id=peer, device_id_type=MESH)

    def picker(step):
        first = jnp.where(owners[step] == me, offsets[step], 4 * here_points)
        row = lax.broadcasted_iota(jnp.int32, (BLOCK, here_points), 0)
        col = lax.broadcasted_iota(jnp.int32, (BLOCK, here_points), 1)
        return jnp.where(col == row + first, 1.0, 0.0).astype(jnp.bfloat16)

    def pick(step, pieces):
        chosen = picker(step)
        dot = lambda a: lax.dot_general(a, chosen, (NT, ((), ())), preferred_element_type=F32)
        high, mid, low = pieces
        to_tiles(spread[step].terms, (dot(high) + dot(mid)) + dot(low))

    for copy in copies[:3]:
        copy.wait()
    pieces = split_three(points[...])
    pick(0, pieces)
    pl.semaphore_wait(barrier, len(peers))
    spread[0].scatter()
    pick(1, pieces)
    spread[0].relay()
    spread[1].scatter()

    cols = points[...].T
    flipped[...] = cols
    cols_norm = jnp.sum(cols * cols, axis=1, keepdims=True)
    for copy in copies[3:]:
        copy.wait()
    padded[...] = jnp.zeros_like(padded)
    padded[:classes] = residual[...]

    spread[0].cross()
    spread[1].relay()
    spread[0].gather()
    spread[1].cross()
    spread[0].forward()
    spread[0].finish()

    eye = (
        lax.broadcasted_iota(jnp.int32, (BLOCK, BLOCK), 0)
        == lax.broadcasted_iota(jnp.int32, (BLOCK, BLOCK), 1)
    ).astype(F32)

    def kernel_tile(left, left_norm, right):
        cross = exact_dot(left, right, NN)
        right_norm = jnp.sum(right * right, axis=0, keepdims=True)
        return jnp.exp(-(left_norm + right_norm - 2.0 * cross) / features)

    def block(step):
        return from_tiles(spread[step].total, features, BLOCK)

    def make_tile(step):
        tiles[step] = kernel_tile(flipped[...], cols_norm, block(step))

    class Inverse:
        def __init__(self, step):
            b = block(step)
            bt = b.T
            gram = kernel_tile(bt, jnp.sum(bt * bt, axis=1, keepdims=True), b) + ridge * eye
            top = jnp.max(jnp.sum(gram, axis=1, keepdims=True), axis=0, keepdims=True)
            centre = 2.0 / (ridge + top)
            err = (top - ridge) / (top + ridge)
            gain = 2.0 / (2.0 - err * err)
            self.gram = gram
            self.value = (gain * centre) * (2.0 * eye - centre * gram)
            self.err = err * err / (2.0 - err * err)

        def gain(self):
            err = self.err
            self.err = err * err / (2.0 - err * err)
            return 2.0 / (2.0 - err * err)

        def rough(self):
            near = self.value.astype(jnp.bfloat16)
            rest = eye - low_dot(self.gram, near)
            self.value = self.gain() * (near.astype(F32) + low_dot(near, rest))

        def fine(self):
            rest = eye - split_dot(self.gram, self.value)
            self.value = self.gain() * (self.value + low_dot(self.value, rest))

        def polish(self):
            rest = eye - exact_dot(self.gram, self.value, NN)
            self.value = self.value + low_dot(self.value, rest)

    def sum_grad(step):
        to_tiles(grads[step].terms, exact_dot(padded[...], tiles[step], NN))
        grads[step].scatter()

    def make_delta(step, inverse):
        grad = from_tiles(grads[step].total, rows, BLOCK)
        square = jnp.sum(jnp.sum(grad * grad, axis=1, keepdims=True), axis=0, keepdims=True)
        scale = step_norm / jnp.sqrt(square / (classes * BLOCK) + 1e-06)
        return scale * exact_dot(grad, inverse, NN)

    def credit(step, delta):
        chosen = picker(step)
        high, mid, low = split_three(delta)
        dot = lambda a: jnp.dot(a, chosen, preferred_element_type=F32)
        return ((dot(high) + dot(mid)) + dot(low))[:classes]

    make_tile(0)
    sum_grad(0)
    inverse = Inverse(0)
    inverse.rough()
    grads[0].cross()
    spread[1].gather()
    inverse.rough()
    inverse.rough()
    inverse.fine()
    grads[0].gather()
    spread[1].forward()
    inverse.fine()
    inverse.polish()
    spread[1].finish()
    make_tile(1)
    grads[0].finish()
    delta = make_delta(0, inverse.value)
    step = split_dot(delta, tiles[0], NT)
    padded[...] = padded[...] - step
    sum_grad(1)
    change[0] = step[:classes]
    change[1] = credit(0, delta)
    inverse = Inverse(1)
    inverse.rough()
    grads[1].cross()
    inverse.rough()
    inverse.rough()
    inverse.fine()
    grads[1].gather()
    inverse.fine()
    inverse.polish()
    grads[1].finish()
    delta = make_delta(1, inverse.value)
    change[0] = change[0] + split_dot(delta, tiles[1], NT)[:classes]
    change[1] = change[1] + credit(1, delta)
    for each in spread + grads:
        each.settle()


def solution(mesh):
    n_group, n_dev = mesh.shape["group"], mesh.shape["dev"]
    layout = Layout(n_group, n_dev)

    def body(points, residual, coeffs, owners, offsets):
        features, here = points.shape
        classes = residual.shape[0]
        rows = -(-classes // SUB) * SUB
        columns = BLOCK // LANES
        blocks_share = layout.share(features // SUB * columns)
        grads_share = layout.share(rows // SUB * columns)
        vmem = pl.BlockSpec(memory_space=pltpu.VMEM)
        anywhere = pl.BlockSpec(memory_space=pl.ANY)
        change = pl.pallas_call(
            functools.partial(kernel, layout, n_group),
            out_shape=jax.ShapeDtypeStruct((2,) + residual.shape, F32),
            in_specs=[anywhere] * 4,
            out_specs=vmem,
            scratch_shapes=[
                pltpu.SMEM(owners.shape, jnp.int32),
                pltpu.SMEM(offsets.shape, jnp.int32),
                pltpu.VMEM(points.shape, F32),
                pltpu.VMEM(residual.shape, F32),
                pltpu.VMEM((rows, here), F32),
                pltpu.VMEM((here, features), F32),
                pltpu.VMEM((2, here, BLOCK), F32),
                pltpu.SemaphoreType.DMA((4,)),
            ]
            + sum_scratch(layout, blocks_share) * 2
            + sum_scratch(layout, grads_share) * 2,
            compiler_params=pltpu.CompilerParams(
                collective_id=0, has_side_effects=True, vmem_limit_bytes=60 * 1024 * 1024
            ),
        )(owners, offsets, points, residual)
        return residual - change[0], coeffs + change[1]

    split = P(None, ("group", "dev"))
    return jax.shard_map(
        body,
        mesh=mesh,
        in_specs=(split, split, split, P(), P()),
        out_specs=(split, split),
        check_vma=False,
    )
```

profile of v0, /device:TPU:0, one launch (start us, length us, event | category | flops | bytes accessed | tf_op | source)
XLA Modules:
  0.0 59.8 jit_solution(3267345818269758406)
XLA Ops:
  0.6 0.0 copy-start
  0.6 0.0 copy-start.1
  0.7 57.2 %shard_map.68 = f32[2,147,512]{2,1,0:T(8,128)} custom-call(s32[2]{0:T(128)} %owners_in.1, s32[2]{0:T(128)} %offsets_in.1, f32[440,512]{1,0:T(8,128)} %points_in.1, f32[147,512]{1,0:T(8,128)} %residual_in.1), custom_call_target="tpu_custom_call" | custom-call | tf_op jit(solution)/shard_map/pallas_call | solution.py:440
  57.8 0.0 copy-done
  57.8 0.0 copy-done.1
  57.8 2.0 %bitcast_add_fusion = (f32[147,512]{1,0:T(8,128)}, f32[147,512]{1,0:T(8,128)}) fusion(f32[147,512]{1,0:T(8,128)S(1)} %copy-done.1, f32[2,147,512]{2,1,0:T(8,128)} %shard_map.68, f32[147,512]{1,0:T(8,128)S(1)} %copy-done), kind=kLoop, calls=%fused_computation | loop fusion | flops 150528 | bytes 1806336 | tf_op jit(solution)/shard_map/add | solution.py:461
Async XLA Ops:
  0.6 57.2 %copy-start = (f32[147,512]{1,0:T(8,128)S(1)}, f32[147,512]{1,0:T(8,128)}, u32[]{:S(2)}) copy-start(f32[147,512]{1,0:T(8,128)} %residual_in.1) | copy-start | bytes 903172
  0.6 57.2 %copy-start.1 = (f32[147,512]{1,0:T(8,128)S(1)}, f32[147,512]{1,0:T(8,128)}, u32[]{:S(2)}) copy-start(f32[147,512]{1,0:T(8,128)} %param.7) | copy-start | bytes 903172
where the time goes:
time: 60 us; the launch traced here: 59.8 us
  Pallas kernels  57.2 us (95%)
  other arithmetic  1.98 us (3%)
  between operations  0.67 us (1%)
    pallas_call x1, Pallas kernels, body(): pl.pallas_call(functools.partial(kernel, layout, n_group), out_shape=jax....  57.2 us
    add x1, other arithmetic, body(): return (residual - change[0], coeffs + change[1])  1.98 us

commit v1 on v0

--- a/solution.py
+++ b/solution.py
@@ -9,6 +9,7 @@
 
 BLOCK = 256
 LANES = 128
+HALVES = BLOCK // LANES
 SUB = 8
 
 ridge = 2.0
@@ -38,6 +39,23 @@
     bl = (b - bh.astype(F32)).astype(jnp.bfloat16)
     dot = lambda u, v: lax.dot_general(u, v, (dims, ((), ())), preferred_element_type=F32)
     return dot(ah, bh) + (dot(ah, bl) + dot(al, bh))
+
+
+def split_two(x):
+    high = x.astype(jnp.bfloat16)
+    return high, (x - high.astype(F32)).astype(jnp.bfloat16)
+
+
+def joined(parts):
+    return parts[0].astype(F32) + parts[1].astype(F32)
+
+
+def cross_dot(left, right):
+    width = right[0].shape[1]
+    both = jnp.concatenate(right, axis=1)
+    out = jnp.dot(left[0], both, preferred_element_type=F32)
+    out = out + jnp.dot(left[1], both, preferred_element_type=F32)
+    return out[:, :width] + out[:, width:]
 
 
 def split_three(x):
@@ -257,7 +275,7 @@
 
 def kernel(layout, n_group, owners_in, offsets_in, points_in, residual_in, change, *scratch):
     owners, offsets, points, residual, padded, flipped, tiles, loads = scratch[:8]
-    sums = [scratch[8 + 6 * i : 14 + 6 * i] for i in range(4)]
+    sums = [scratch[8 + 6 * i : 14 + 6 * i] for i in range(2 * HALVES + 2)]
     group, dev = lax.axis_index("group"), lax.axis_index("dev")
     me = group * layout.n_dev + dev
     features, here_points = points.shape
@@ -274,10 +292,12 @@
         copy.start()
 
     blocks_share = sums[0][2].shape[0]
-    grads_share = sums[2][2].shape[0]
+    grads_share = sums[-1][2].shape[0]
     BlockSum = PairedSum if layout.cores == 2 else Sum
-    spread = [BlockSum(layout, (group, dev), blocks_share, sums[i]) for i in range(2)]
-    grads = [Sum(layout, (group, dev), grads_share, sums[2 + i]) for i in range(2)]
+    at = (group, dev)
+    spread = [BlockSum(layout, at, blocks_share, refs) for refs in sums[: 2 * HALVES]]
+    grads = [Sum(layout, at, grads_share, refs) for refs in sums[2 * HALVES :]]
+    left0, right0, left1, right1 = spread
 
     barrier = pltpu.get_barrier_semaphore()
     peers = [grads[0].peer_in_plane(k)[1] for k in range(1, layout.plane)]
@@ -291,36 +311,46 @@
         col = lax.broadcasted_iota(jnp.int32, (BLOCK, here_points), 1)
         return jnp.where(col == row + first, 1.0, 0.0).astype(jnp.bfloat16)
 
-    def pick(step, pieces):
-        chosen = picker(step)
+    def pick(index):
+        chosen = picker(index // HALVES)
+        at = index % HALVES * LANES
+        chosen = chosen[at : at + LANES]
         dot = lambda a: lax.dot_general(a, chosen, (NT, ((), ())), preferred_element_type=F32)
         high, mid, low = pieces
-        to_tiles(spread[step].terms, (dot(high) + dot(mid)) + dot(low))
+        to_tiles(spread[index].terms, (dot(high) + dot(mid)) + dot(low))
 
     for copy in copies[:3]:
         copy.wait()
     pieces = split_three(points[...])
-    pick(0, pieces)
+    pick(0)
     pl.semaphore_wait(barrier, len(peers))
-    spread[0].scatter()
-    pick(1, pieces)
-    spread[0].relay()
-    spread[1].scatter()
-
-    cols = points[...].T
-    flipped[...] = cols
+    left0.scatter()
+    pick(1)
+    left0.relay()
+    right0.scatter()
+    pick(2)
+    left0.cross()
+    right0.relay()
+    left1.scatter()
+    pick(3)
+
+    cols = split_two(points[...].T)
+    flipped[0], flipped[1] = cols
+    cols = joined(cols)
     cols_norm = jnp.sum(cols * cols, axis=1, keepdims=True)
     for copy in copies[3:]:
         copy.wait()
     padded[...] = jnp.zeros_like(padded)
     padded[:classes] = residual[...]
 
-    spread[0].cross()
-    spread[1].relay()
-    spread[0].gather()
-    spread[1].cross()
-    spread[0].forward()
-    spread[0].finish()
+    left0.gather()
+    right0.cross()
+    left1.relay()
+    right1.scatter()
+    left0.forward()
+    right0.gather()
+    left1.cross()
+    right1.relay()
 
     eye = (
         lax.broadcasted_iota(jnp.int32, (BLOCK, BLOCK), 0)
@@ -328,21 +358,28 @@
     ).astype(F32)
 
     def kernel_tile(left, left_norm, right):
-        cross = exact_dot(left, right, NN)
-        right_norm = jnp.sum(right * right, axis=0, keepdims=True)
-        return jnp.exp(-(left_norm + right_norm - 2.0 * cross) / features)
-
-    def block(step):
-        return from_tiles(spread[step].total, features, BLOCK)
-
-    def make_tile(step):
-        tiles[step] = kernel_tile(flipped[...], cols_norm, block(step))
+        right = split_two(right)
+        whole = joined(right)
+        right_norm = jnp.sum(whole * whole, axis=0, keepdims=True)
+        return jnp.exp(-(left_norm + right_norm - 2.0 * cross_dot(left, right)) / features)
+
+    def half_block(index):
+        return from_tiles(spread[index].total, features, LANES)
+
+    def half_tile(index):
+        spread[index].finish()
+        at = index % HALVES * LANES
+        tiles[index // HALVES, :, at : at + LANES] = kernel_tile(
+            (flipped[0], flipped[1]), cols_norm, half_block(index)
+        )
 
     class Inverse:
         def __init__(self, step):
-            b = block(step)
-            bt = b.T
-            gram = kernel_tile(bt, jnp.sum(bt * bt, axis=1, keepdims=True), b) + ridge * eye
+            halves = [half_block(HALVES * step + h) for h in range(HALVES)]
+            b = jnp.concatenate(halves, axis=1)
+            rows = split_two(b.T)
+            whole = joined(rows)
+            gram = kernel_tile(rows, jnp.sum(whole * whole, axis=1, keepdims=True), b) + ridge * eye
             top = jnp.max(jnp.sum(gram, axis=1, keepdims=True), axis=0, keepdims=True)
             centre = 2.0 / (ridge + top)
             err = (top - ridge) / (top + ridge)
@@ -385,21 +422,26 @@
         dot = lambda a: jnp.dot(a, chosen, preferred_element_type=F32)
         return ((dot(high) + dot(mid)) + dot(low))[:classes]
 
-    make_tile(0)
+    half_tile(0)
+    right0.forward()
+    right1.cross()
+    half_tile(1)
     sum_grad(0)
     inverse = Inverse(0)
     inverse.rough()
     grads[0].cross()
-    spread[1].gather()
+    left1.gather()
+    right1.gather()
     inverse.rough()
     inverse.rough()
     inverse.fine()
+    left1.forward()
+    right1.forward()
     grads[0].gather()
-    spread[1].forward()
     inverse.fine()
     inverse.polish()
-    spread[1].finish()
-    make_tile(1)
+    half_tile(2)
+    half_tile(3)
     grads[0].finish()
     delta = make_delta(0, inverse.value)
     step = split_dot(delta, tiles[0], NT)
@@ -432,9 +474,8 @@
         features, here = points.shape
         classes = residual.shape[0]
         rows = -(-classes // SUB) * SUB
-        columns = BLOCK // LANES
-        blocks_share = layout.share(features // SUB * columns)
-        grads_share = layout.share(rows // SUB * columns)
+        blocks_share = layout.share(features // SUB)
+        grads_share = layout.share(rows // SUB * HALVES)
         vmem = pl.BlockSpec(memory_space=pltpu.VMEM)
         anywhere = pl.BlockSpec(memory_space=pl.ANY)
         change = pl.pallas_call(
@@ -448,11 +489,11 @@
                 pltpu.VMEM(points.shape, F32),
                 pltpu.VMEM(residual.shape, F32),
                 pltpu.VMEM((rows, here), F32),
-                pltpu.VMEM((here, features), F32),
+                pltpu.VMEM((2, here, features), jnp.bfloat16),
                 pltpu.VMEM((2, here, BLOCK), F32),
                 pltpu.SemaphoreType.DMA((4,)),
             ]
-            + sum_scratch(layout, blocks_share) * 2
+            + sum_scratch(layout, blocks_share) * (2 * HALVES)
             + sum_scratch(layout, grads_share) * 2,
             compiler_params=pltpu.CompilerParams(
                 collective_id=0, has_side_effects=True, vmem_limit_bytes=60 * 1024 * 1024

time: 60 us -> 59.7 us (level)
  no operation moved by 1% of the time
where the time goes in v1:
time: 59.7 us; the launch traced here: 59.5 us
  Pallas kernels  56.8 us (95%)
  other arithmetic  1.98 us (3%)
  between operations  0.67 us (1%)
    pallas_call x1, Pallas kernels, body(): pl.pallas_call(functools.partial(kernel, layout, n_group), out_shape=jax....  56.8 us
    add x1, other arithmetic, body(): return (residual - change[0], coeffs + change[1])  1.98 us

profile of v1, /device:TPU:0, one launch (start us, length us, event | category | flops | bytes accessed | tf_op | source)
XLA Modules:
  0.0 59.5 jit_solution(7269193291964741082)
XLA Ops:
  0.6 0.0 copy-start
  0.6 0.0 copy-start.1
  0.7 56.8 %shard_map.68 = f32[2,147,512]{2,1,0:T(8,128)} custom-call(s32[2]{0:T(128)} %owners_in.1, s32[2]{0:T(128)} %offsets_in.1, f32[440,512]{1,0:T(8,128)} %points_in.1, f32[147,512]{1,0:T(8,128)} %residual_in.1), custom_call_target="tpu_custom_call" | custom-call | tf_op jit(solution)/shard_map/pallas_call | solution.py:481
  57.5 0.0 copy-done
  57.5 0.0 copy-done.1
  57.5 2.0 %bitcast_add_fusion = (f32[147,512]{1,0:T(8,128)}, f32[147,512]{1,0:T(8,128)}) fusion(f32[147,512]{1,0:T(8,128)S(1)} %copy-done.1, f32[2,147,512]{2,1,0:T(8,128)} %shard_map.68, f32[147,512]{1,0:T(8,128)S(1)} %copy-done), kind=kLoop, calls=%fused_computation | loop fusion | flops 150528 | bytes 1806336 | tf_op jit(solution)/shard_map/add | solution.py:502
Async XLA Ops:
  0.6 56.9 %copy-start = (f32[147,512]{1,0:T(8,128)S(1)}, f32[147,512]{1,0:T(8,128)}, u32[]{:S(2)}) copy-start(f32[147,512]{1,0:T(8,128)} %residual_in.1) | copy-start | bytes 903172
  0.6 56.9 %copy-start.1 = (f32[147,512]{1,0:T(8,128)S(1)}, f32[147,512]{1,0:T(8,128)}, u32[]{:S(2)}) copy-start(f32[147,512]{1,0:T(8,128)} %param.7) | copy-start | bytes 903172

commit v2 on v1

--- a/solution.py
+++ b/solution.py
@@ -92,7 +92,7 @@
         self.terms, self.landed, self.held, self.crossed, self.total, self.sems = refs
         self.place = self.group * layout.width + lax.rem(self.dev, layout.width)
         self.plane = self.dev // layout.width
-        self.started = []
+        self.sent = {}
 
     def peer_in_plane(self, k):
         to = lax.rem(self.place + k, self.layout.plane)
@@ -107,51 +107,45 @@
     def piece(self, index):
         return pl.ds(index * self.share, self.share)
 
-    def send(self, src, dst, sem, to):
-        copy = pltpu.make_async_remote_copy(
+    def send(self, src, dst, to, out_sem, in_sem):
+        pltpu.make_async_remote_copy(
             src_ref=src,
             dst_ref=dst,
-            send_sem=self.sems.at[0, sem],
-            recv_sem=self.sems.at[1, sem],
+            send_sem=self.sems.at[0, out_sem],
+            recv_sem=self.sems.at[1, in_sem],
             device_id=to,
             device_id_type=MESH,
-        )
-        copy.start()
-        self.waiting.append(copy)
-
-    def arrive(self):
-        for copy in self.waiting:
-            copy.wait_recv()
-        self.started += self.waiting
+        ).start()
+        self.sent[out_sem] = self.sent.get(out_sem, 0) + 1
+
+    def wait(self, way, sem, count):
+        if count:
+            like = self.terms.at[pl.ds(0, count * self.share)]
+            pltpu.make_async_copy(like, like, self.sems.at[way, sem]).wait()
 
     def scatter(self):
-        self.waiting = []
         for k in range(1, self.layout.plane):
             to, device = self.peer_in_plane(k)
-            self.send(self.terms.at[self.piece(to)], self.landed.at[self.piece(k - 1)], k - 1, device)
+            self.send(self.terms.at[self.piece(to)], self.landed.at[self.piece(k - 1)], device, 0, 0)
 
     def cross(self):
-        self.arrive()
+        self.wait(1, 0, self.layout.plane - 1)
         total = self.terms[self.piece(self.place)]
         for k in range(self.layout.plane - 1):
             total = total + self.landed[self.piece(k)]
         self.held[...] = total
-        self.waiting = []
-        first = self.layout.plane - 1
         for k in range(1, self.layout.line):
-            self.send(self.held, self.crossed.at[self.piece(k - 1)], first + k - 1, self.peer_in_line(k))
+            self.send(self.held, self.crossed.at[self.piece(k - 1)], self.peer_in_line(k), 1, 1)
 
     def gather(self):
-        self.arrive()
+        self.wait(1, 1, self.layout.line - 1)
+        mine = self.total.at[self.piece(self.place)]
         total = self.held[...]
         for k in range(self.layout.line - 1):
             total = total + self.crossed[self.piece(k)]
-        mine = self.total.at[self.piece(self.place)]
         mine[...] = total
-        self.waiting = []
-        first = self.layout.plane + self.layout.line - 2
         for k in range(1, self.layout.plane):
-            self.send(mine, mine, first + k - 1, self.peer_in_plane(k)[1])
+            self.send(mine, mine, self.peer_in_plane(k)[1], 2, 2)
 
     def relay(self):
         pass
@@ -160,11 +154,11 @@
         pass
 
     def finish(self):
-        self.arrive()
+        self.wait(1, 2, self.layout.plane - 1)
 
     def settle(self):
-        for copy in self.started:
-            copy.wait_send()
+        for sem, count in sorted(self.sent.items()):
+            self.wait(0, sem, count)
 
 
 class PairedSum(Sum):
@@ -185,74 +179,66 @@
         return to, (group, self.plane * layout.width + lax.rem(to, layout.width))
 
     def scatter(self):
-        layout = self.layout
-        self.waiting = []
-        for k in range(1, layout.chips + 1):
-            to = (1 - self.core) * layout.chips + lax.rem(self.chip + k, layout.chips)
-            self.send(self.terms.at[self.piece(to)], self.landed.at[self.piece(k - 1)], k - 1, self.sibling())
+        chips = self.layout.chips
+        for k in range(1, chips + 1):
+            to = (1 - self.core) * chips + lax.rem(self.chip + k, chips)
+            src, dst = self.terms.at[self.piece(to)], self.landed.at[self.piece(k - 1)]
+            self.send(src, dst, self.sibling(), 0, k - 1)
 
     def relay(self):
-        layout = self.layout
-        pairs, self.waiting = self.waiting, []
-        for k in range(1, layout.chips + 1):
-            pairs[k - 1].wait_recv()
+        chips = self.layout.chips
+        for k in range(1, chips + 1):
+            self.wait(1, k - 1, 1)
             to, device = self.other_chip(k)
-            mine = self.piece(self.core * layout.chips + to)
+            mine = self.piece(self.core * chips + to)
             self.terms[mine] = self.terms[mine] + self.landed[self.piece(k - 1)]
-            if k < layout.chips:
-                slot = layout.chips + k - 1
-                self.send(self.terms.at[mine], self.landed.at[self.piece(slot)], slot, device)
-        self.started += pairs
+            if k < chips:
+                self.send(self.terms.at[mine], self.landed.at[self.piece(chips + k - 1)], device, 1, chips)
 
     def cross(self):
-        layout = self.layout
-        self.arrive()
+        layout, chips = self.layout, self.layout.chips
+        self.wait(1, chips, chips - 1)
         total = self.terms[self.piece(self.place)]
-        for k in range(1, layout.chips):
-            total = total + self.landed[self.piece(layout.chips + k - 1)]
+        for k in range(1, chips):
+            total = total + self.landed[self.piece(chips + k - 1)]
         self.held[...] = total
-        self.waiting = []
-        first = layout.plane - 1
         for k in range(1, layout.line):
-            self.send(self.held, self.crossed.at[self.piece(k - 1)], first + k - 1, self.peer_in_line(k))
+            self.send(self.held, self.crossed.at[self.piece(k - 1)], self.peer_in_line(k), 2, chips + 1)
 
     def gather(self):
-        layout = self.layout
-        self.arrive()
+        layout, chips = self.layout, self.layout.chips
+        self.wait(1, chips + 1, layout.line - 1)
         total = self.held[...]
         for k in range(layout.line - 1):
             total = total + self.crossed[self.piece(k)]
         mine = self.total.at[self.piece(self.place)]
         mine[...] = total
-        self.waiting = []
-        first = layout.plane + layout.line - 2
-        for k in range(1, layout.chips):
-            self.send(mine, mine, first + k - 1, self.other_chip(k)[1])
-        chips, self.waiting = self.waiting, []
-        self.send(mine, mine, first + layout.chips - 1, self.sibling())
-        self.chip_copies = chips
+        for k in range(1, chips):
+            self.send(mine, mine, self.other_chip(k)[1], 3, chips + 1 + k)
+        self.send(mine, mine, self.sibling(), 4, 2 * chips + 1)
 
     def forward(self):
-        layout = self.layout
-        first = layout.plane + layout.line - 2 + layout.chips - 1
-        for k in range(1, layout.chips):
-            self.chip_copies[k - 1].wait_recv()
-            source = lax.rem(self.chip + layout.chips - k, layout.chips)
-            where = self.total.at[self.piece(self.core * layout.chips + source)]
-            self.send(where, where, first + k, self.sibling())
-        self.started += self.chip_copies
+        chips = self.layout.chips
+        for k in range(1, chips):
+            self.wait(1, chips + 1 + k, 1)
+            source = lax.rem(self.chip + chips - k, chips)
+            where = self.total.at[self.piece(self.core * chips + source)]
+            self.send(where, where, self.sibling(), 4, 2 * chips + 1)
+
+    def finish(self):
+        self.wait(1, 2 * self.layout.chips + 1, self.layout.chips)
 
 
 def sum_scratch(layout, share):
     tile = (SUB, LANES)
-    copies = 2 * layout.plane + layout.line - 1
+    sems = 2 * layout.chips + 5
     return [
         pltpu.VMEM((layout.plane * share,) + tile, F32),
         pltpu.VMEM((max(layout.plane - 1, 1) * share,) + tile, F32),
         pltpu.VMEM((share,) + tile, F32),
         pltpu.VMEM((max(layout.line - 1, 1) * share,) + tile, F32),
         pltpu.VMEM((layout.plane * share,) + tile, F32),
-        pltpu.SemaphoreType.DMA((2, copies)),
+        pltpu.SemaphoreType.DMA((2, sems)),
     ]
 
 
@@ -328,28 +314,26 @@
     pick(1)
     left0.relay()
     right0.scatter()
-    pick(2)
-    left0.cross()
-    right0.relay()
-    left1.scatter()
-    pick(3)
-
     cols = split_two(points[...].T)
     flipped[0], flipped[1] = cols
+    right0.relay()
+    left0.cross()
     cols = joined(cols)
     cols_norm = jnp.sum(cols * cols, axis=1, keepdims=True)
+    right0.cross()
+    pick(2)
+    left1.scatter()
     for copy in copies[3:]:
         copy.wait()
     padded[...] = jnp.zeros_like(padded)
     padded[:classes] = residual[...]
-
     left0.gather()
-    right0.cross()
     left1.relay()
+    pick(3)
     right1.scatter()
-    left0.forward()
     right0.gather()
     left1.cross()
+    left0.forward()
     right1.relay()
 
     eye = (
@@ -452,6 +436,9 @@
     inverse = Inverse(1)
     inverse.rough()
     grads[1].cross()
+    for each in spread:
+        each.settle()
+    grads[0].settle()
     inverse.rough()
     inverse.rough()
     inverse.fine()
@@ -462,8 +449,7 @@
     delta = make_delta(1, inverse.value)
     change[0] = change[0] + split_dot(delta, tiles[1], NT)[:classes]
     change[1] = change[1] + credit(1, delta)
-    for each in spread + grads:
-        each.settle()
+    grads[1].settle()
 
 
 def solution(mesh):

time: 59.7 us -> 58.4 us (0.978)
  Pallas kernels: 56.8 us -> 55.5 us
    pallas_call x1, Pallas kernels: 56.8 us -> 55.5 us  [body(): pl.pallas_call(functools.partial(kernel, layout, n_group), out_shape=jax....]
where the time goes in v2:
time: 58.4 us; the launch traced here: 58.2 us
  Pallas kernels  55.5 us (95%)
  other arithmetic  1.98 us (3%)
  between operations  0.67 us (1%)
    pallas_call x1, Pallas kernels, body(): pl.pallas_call(functools.partial(kernel, layout, n_group), out_shape=jax....  55.5 us
    add x1, other arithmetic, body(): return (residual - change[0], coeffs + change[1])  1.98 us

profile of v2, /device:TPU:0, one launch (start us, length us, event | category | flops | bytes accessed | tf_op | source)
XLA Modules:
  0.0 58.2 jit_solution(4300785102548374341)
XLA Ops:
  0.6 0.0 copy-start
  0.6 0.0 copy-start.1
  0.7 55.5 %shard_map.68 = f32[2,147,512]{2,1,0:T(8,128)} custom-call(s32[2]{0:T(128)} %owners_in.1, s32[2]{0:T(128)} %offsets_in.1, f32[440,512]{1,0:T(8,128)} %points_in.1, f32[147,512]{1,0:T(8,128)} %residual_in.1), custom_call_target="tpu_custom_call" | custom-call | tf_op jit(solution)/shard_map/pallas_call | solution.py:467
  56.2 0.0 copy-done
  56.2 0.0 copy-done.1
  56.2 2.0 %bitcast_add_fusion = (f32[147,512]{1,0:T(8,128)}, f32[147,512]{1,0:T(8,128)}) fusion(f32[147,512]{1,0:T(8,128)S(1)} %copy-done.1, f32[2,147,512]{2,1,0:T(8,128)} %shard_map.68, f32[147,512]{1,0:T(8,128)S(1)} %copy-done), kind=kLoop, calls=%fused_computation | loop fusion | flops 150528 | bytes 1806336 | tf_op jit(solution)/shard_map/add | solution.py:488
Async XLA Ops:
  0.6 55.6 %copy-start = (f32[147,512]{1,0:T(8,128)S(1)}, f32[147,512]{1,0:T(8,128)}, u32[]{:S(2)}) copy-start(f32[147,512]{1,0:T(8,128)} %residual_in.1) | copy-start | bytes 903172
  0.6 55.6 %copy-start.1 = (f32[147,512]{1,0:T(8,128)S(1)}, f32[147,512]{1,0:T(8,128)}, u32[]{:S(2)}) copy-start(f32[147,512]{1,0:T(8,128)} %param.7) | copy-start | bytes 903172

commit v3 on v2

--- a/solution.py
+++ b/solution.py
@@ -107,7 +107,7 @@
     def piece(self, index):
         return pl.ds(index * self.share, self.share)
 
-    def send(self, src, dst, to, out_sem, in_sem):
+    def send(self, src, dst, to, out_sem, in_sem, pieces=1):
         pltpu.make_async_remote_copy(
             src_ref=src,
             dst_ref=dst,
@@ -116,7 +116,7 @@
             device_id=to,
             device_id_type=MESH,
         ).start()
-        self.sent[out_sem] = self.sent.get(out_sem, 0) + 1
+        self.sent[out_sem] = self.sent.get(out_sem, 0) + pieces
 
     def wait(self, way, sem, count):
         if count:
@@ -178,67 +178,65 @@
         group = (to // layout.width) * layout.cores + self.core
         return to, (group, self.plane * layout.width + lax.rem(to, layout.width))
 
+    def share_of(self, core):
+        chips = self.layout.chips
+        return pl.ds(core * chips * self.share, chips * self.share)
+
     def scatter(self):
         chips = self.layout.chips
-        for k in range(1, chips + 1):
-            to = (1 - self.core) * chips + lax.rem(self.chip + k, chips)
-            src, dst = self.terms.at[self.piece(to)], self.landed.at[self.piece(k - 1)]
-            self.send(src, dst, self.sibling(), 0, k - 1)
+        src, dst = self.terms.at[self.share_of(1 - self.core)], self.landed.at[: chips * self.share]
+        self.send(src, dst, self.sibling(), 0, 0, chips)
 
     def relay(self):
         chips = self.layout.chips
-        for k in range(1, chips + 1):
-            self.wait(1, k - 1, 1)
+        self.wait(1, 0, chips)
+        mine = self.share_of(self.core)
+        self.terms[mine] = self.terms[mine] + self.landed[: chips * self.share]
+        for k in range(1, chips):
             to, device = self.other_chip(k)
-            mine = self.piece(self.core * chips + to)
-            self.terms[mine] = self.terms[mine] + self.landed[self.piece(k - 1)]
-            if k < chips:
-                self.send(self.terms.at[mine], self.landed.at[self.piece(chips + k - 1)], device, 1, chips)
+            src = self.terms.at[self.piece(self.core * chips + to)]
+            self.send(src, self.landed.at[self.piece(chips + k - 1)], device, 1, 1)
 
     def cross(self):
         layout, chips = self.layout, self.layout.chips
-        self.wait(1, chips, chips - 1)
+        self.wait(1, 1, chips - 1)
         total = self.terms[self.piece(self.place)]
         for k in range(1, chips):
             total = total + self.landed[self.piece(chips + k - 1)]
         self.held[...] = total
         for k in range(1, layout.line):
-            self.send(self.held, self.crossed.at[self.piece(k - 1)], self.peer_in_line(k), 2, chips + 1)
+            self.send(self.held, self.crossed.at[self.piece(k - 1)], self.peer_in_line(k), 2, 2)
 
     def gather(self):
         layout, chips = self.layout, self.layout.chips
-        self.wait(1, chips + 1, layout.line - 1)
+        self.wait(1, 2, layout.line - 1)
         total = self.held[...]
         for k in range(layout.line - 1):
             total = total + self.crossed[self.piece(k)]
         mine = self.total.at[self.piece(self.place)]
         mine[...] = total
         for k in range(1, chips):
-            self.send(mine, mine, self.other_chip(k)[1], 3, chips + 1 + k)
-        self.send(mine, mine, self.sibling(), 4, 2 * chips + 1)
+            self.send(mine, mine, self.other_chip(k)[1], 3, 3)
 
     def forward(self):
         chips = self.layout.chips
-        for k in range(1, chips):
-            self.wait(1, chips + 1 + k, 1)
-            source = lax.rem(self.chip + chips - k, chips)
-            where = self.total.at[self.piece(self.core * chips + source)]
-            self.send(where, where, self.sibling(), 4, 2 * chips + 1)
+        self.wait(1, 3, chips - 1)
+        mine = self.total.at[self.share_of(self.core)]
+        self.send(mine, mine, self.sibling(), 4, 4, chips)
 
     def finish(self):
-        self.wait(1, 2 * self.layout.chips + 1, self.layout.chips)
+        self.wait(1, 4, self.layout.chips)
 
 
 def sum_scratch(layout, share):
     tile = (SUB, LANES)
-    sems = 2 * layout.chips + 5
     return [
         pltpu.VMEM((layout.plane * share,) + tile, F32),
         pltpu.VMEM((max(layout.plane - 1, 1) * share,) + tile, F32),
         pltpu.VMEM((share,) + tile, F32),
         pltpu.VMEM((max(layout.line - 1, 1) * share,) + tile, F32),
         pltpu.VMEM((layout.plane * share,) + tile, F32),
-        pltpu.SemaphoreType.DMA((2, sems)),
+        pltpu.SemaphoreType.DMA((2, 5)),
     ]
 
 
@@ -419,13 +417,13 @@
     inverse.rough()
     inverse.rough()
     inverse.fine()
+    grads[0].gather()
     left1.forward()
     right1.forward()
-    grads[0].gather()
     inverse.fine()
-    inverse.polish()
     half_tile(2)
     half_tile(3)
+    inverse.polish()
     grads[0].finish()
     delta = make_delta(0, inverse.value)
     step = split_dot(delta, tiles[0], NT)
@@ -463,11 +461,11 @@
         blocks_share = layout.share(features // SUB)
         grads_share = layout.share(rows // SUB * HALVES)
         vmem = pl.BlockSpec(memory_space=pltpu.VMEM)
-        anywhere = pl.BlockSpec(memory_space=pl.ANY)
+        outside = pl.BlockSpec(memory_space=pltpu.HBM)
         change = pl.pallas_call(
             functools.partial(kernel, layout, n_group),
             out_shape=jax.ShapeDtypeStruct((2,) + residual.shape, F32),
-            in_specs=[anywhere] * 4,
+            in_specs=[outside] * 4,
             out_specs=vmem,
             scratch_shapes=[
                 pltpu.SMEM(owners.shape, jnp.int32),

time: 58.4 us -> 55.6 us (0.952)
  Pallas kernels: 55.5 us -> 52.8 us
    pallas_call x1, Pallas kernels: 55.5 us -> 52.8 us  [body(): pl.pallas_call(functools.partial(kernel, layout, n_group), out_shape=jax....]
where the time goes in v3:
time: 55.6 us; the launch traced here: 55.4 us
  Pallas kernels  52.8 us (95%)
  other arithmetic  1.98 us (4%)
  between operations  0.67 us (1%)
    pallas_call x1, Pallas kernels, body(): pl.pallas_call(functools.partial(kernel, layout, n_group), out_shape=jax....  52.8 us
    add x1, other arithmetic, body(): return (residual - change[0], coeffs + change[1])  1.98 us

profile of v3, /device:TPU:0, one launch (start us, length us, event | category | flops | bytes accessed | tf_op | source)
XLA Modules:
  0.0 55.4 jit_solution(4234143266322812949)
XLA Ops:
  0.6 0.0 copy-start
  0.6 0.0 copy-start.1
  0.7 52.8 %shard_map.68 = f32[2,147,512]{2,1,0:T(8,128)} custom-call(s32[2]{0:T(128)} %owners_in.1, s32[2]{0:T(128)} %offsets_in.1, f32[440,512]{1,0:T(8,128)} %points_in.1, f32[147,512]{1,0:T(8,128)} %residual_in.1), custom_call_target="tpu_custom_call" | custom-call | tf_op jit(solution)/shard_map/pallas_call | solution.py:465
  53.4 0.0 copy-done
  53.4 0.0 copy-done.1
  53.5 2.0 %bitcast_add_fusion = (f32[147,512]{1,0:T(8,128)}, f32[147,512]{1,0:T(8,128)}) fusion(f32[147,512]{1,0:T(8,128)S(1)} %copy-done.1, f32[2,147,512]{2,1,0:T(8,128)} %shard_map.68, f32[147,512]{1,0:T(8,128)S(1)} %copy-done), kind=kLoop, calls=%fused_computation | loop fusion | flops 150528 | bytes 1806336 | tf_op jit(solution)/shard_map/add | solution.py:486
Async XLA Ops:
  0.6 52.8 %copy-start = (f32[147,512]{1,0:T(8,128)S(1)}, f32[147,512]{1,0:T(8,128)}, u32[]{:S(2)}) copy-start(f32[147,512]{1,0:T(8,128)} %residual_in.1) | copy-start | bytes 903172
  0.6 52.8 %copy-start.1 = (f32[147,512]{1,0:T(8,128)S(1)}, f32[147,512]{1,0:T(8,128)}, u32[]{:S(2)}) copy-start(f32[147,512]{1,0:T(8,128)} %param.7) | copy-start | bytes 903172

commit v4 on v3

--- a/solution.py
+++ b/solution.py
@@ -259,7 +259,7 @@
 
 def kernel(layout, n_group, owners_in, offsets_in, points_in, residual_in, change, *scratch):
     owners, offsets, points, residual, padded, flipped, tiles, loads = scratch[:8]
-    sums = [scratch[8 + 6 * i : 14 + 6 * i] for i in range(2 * HALVES + 2)]
+    sums = [scratch[8 + 6 * i : 14 + 6 * i] for i in range(HALVES + 3)]
     group, dev = lax.axis_index("group"), lax.axis_index("dev")
     me = group * layout.n_dev + dev
     features, here_points = points.shape
@@ -275,13 +275,11 @@
     for copy in copies:
         copy.start()
 
-    blocks_share = sums[0][2].shape[0]
-    grads_share = sums[-1][2].shape[0]
     BlockSum = PairedSum if layout.cores == 2 else Sum
     at = (group, dev)
-    spread = [BlockSum(layout, at, blocks_share, refs) for refs in sums[: 2 * HALVES]]
-    grads = [Sum(layout, at, grads_share, refs) for refs in sums[2 * HALVES :]]
-    left0, right0, left1, right1 = spread
+    spread = [BlockSum(layout, at, refs[2].shape[0], refs) for refs in sums[: HALVES + 1]]
+    grads = [Sum(layout, at, refs[2].shape[0], refs) for refs in sums[HALVES + 1 :]]
+    left0, right0, second = spread
 
     barrier = pltpu.get_barrier_semaphore()
     peers = [grads[0].peer_in_plane(k)[1] for k in range(1, layout.plane)]
@@ -295,21 +293,19 @@
         col = lax.broadcasted_iota(jnp.int32, (BLOCK, here_points), 1)
         return jnp.where(col == row + first, 1.0, 0.0).astype(jnp.bfloat16)
 
-    def pick(index):
-        chosen = picker(index // HALVES)
-        at = index % HALVES * LANES
-        chosen = chosen[at : at + LANES]
+    def pick(target, chosen):
         dot = lambda a: lax.dot_general(a, chosen, (NT, ((), ())), preferred_element_type=F32)
         high, mid, low = pieces
-        to_tiles(spread[index].terms, (dot(high) + dot(mid)) + dot(low))
+        to_tiles(target.terms, (dot(high) + dot(mid)) + dot(low))
 
     for copy in copies[:3]:
         copy.wait()
     pieces = split_three(points[...])
-    pick(0)
+    chosen = picker(0)
+    pick(left0, chosen[:LANES])
     pl.semaphore_wait(barrier, len(peers))
     left0.scatter()
-    pick(1)
+    pick(right0, chosen[LANES:])
     left0.relay()
     right0.scatter()
     cols = split_two(points[...].T)
@@ -319,20 +315,16 @@
     cols = joined(cols)
     cols_norm = jnp.sum(cols * cols, axis=1, keepdims=True)
     right0.cross()
-    pick(2)
-    left1.scatter()
+    pick(second, picker(1))
+    second.scatter()
     for copy in copies[3:]:
         copy.wait()
     padded[...] = jnp.zeros_like(padded)
     padded[:classes] = residual[...]
     left0.gather()
-    left1.relay()
-    pick(3)
-    right1.scatter()
+    second.relay()
     right0.gather()
-    left1.cross()
     left0.forward()
-    right1.relay()
 
     eye = (
         lax.broadcasted_iota(jnp.int32, (BLOCK, BLOCK), 0)
@@ -345,20 +337,21 @@
         right_norm = jnp.sum(whole * whole, axis=0, keepdims=True)
         return jnp.exp(-(left_norm + right_norm - 2.0 * cross_dot(left, right)) / features)
 
-    def half_block(index):
-        return from_tiles(spread[index].total, features, LANES)
-
-    def half_tile(index):
-        spread[index].finish()
-        at = index % HALVES * LANES
-        tiles[index // HALVES, :, at : at + LANES] = kernel_tile(
-            (flipped[0], flipped[1]), cols_norm, half_block(index)
+    def block(step):
+        if step:
+            return from_tiles(second.total, features, BLOCK)
+        halves = [from_tiles(half.total, features, LANES) for half in (left0, right0)]
+        return jnp.concatenate(halves, axis=1)
+
+    def make_tile(step, source, first, width):
+        source.finish()
+        tiles[step, :, first : first + width] = kernel_tile(
+            (flipped[0], flipped[1]), cols_norm, from_tiles(source.total, features, width)
         )
 
     class Inverse:
         def __init__(self, step):
-            halves = [half_block(HALVES * step + h) for h in range(HALVES)]
-            b = jnp.concatenate(halves, axis=1)
+            b = block(step)
             rows = split_two(b.T)
             whole = joined(rows)
             gram = kernel_tile(rows, jnp.sum(whole * whole, axis=1, keepdims=True), b) + ridge * eye
@@ -404,26 +397,23 @@
         dot = lambda a: jnp.dot(a, chosen, preferred_element_type=F32)
         return ((dot(high) + dot(mid)) + dot(low))[:classes]
 
-    half_tile(0)
+    make_tile(0, left0, 0, LANES)
+    second.cross()
     right0.forward()
-    right1.cross()
-    half_tile(1)
+    make_tile(0, right0, LANES, LANES)
     sum_grad(0)
     inverse = Inverse(0)
     inverse.rough()
     grads[0].cross()
-    left1.gather()
-    right1.gather()
-    inverse.rough()
-    inverse.rough()
+    second.gather()
+    inverse.rough()
+    inverse.rough()
+    inverse.fine()
     inverse.fine()
     grads[0].gather()
-    left1.forward()
-    right1.forward()
-    inverse.fine()
-    half_tile(2)
-    half_tile(3)
+    second.forward()
     inverse.polish()
+    make_tile(1, second, 0, BLOCK)
     grads[0].finish()
     delta = make_delta(0, inverse.value)
     step = split_dot(delta, tiles[0], NT)
@@ -458,7 +448,8 @@
         features, here = points.shape
         classes = residual.shape[0]
         rows = -(-classes // SUB) * SUB
-        blocks_share = layout.share(features // SUB)
+        half_share = layout.share(features // SUB)
+        block_share = layout.share(features // SUB * HALVES)
         grads_share = layout.share(rows // SUB * HALVES)
         vmem = pl.BlockSpec(memory_space=pltpu.VMEM)
         outside = pl.BlockSpec(memory_space=pltpu.HBM)
@@ -477,7 +468,8 @@
                 pltpu.VMEM((2, here, BLOCK), F32),
                 pltpu.SemaphoreType.DMA((4,)),
             ]
-            + sum_scratch(layout, blocks_share) * (2 * HALVES)
+            + sum_scratch(layout, half_share) * HALVES
+            + sum_scratch(layout, block_share)
             + sum_scratch(layout, grads_share) * 2,
             compiler_params=pltpu.CompilerParams(
                 collective_id=0, has_side_effects=True, vmem_limit_bytes=60 * 1024 * 1024

time: 55.6 us -> 57.5 us (1.034)
  Pallas kernels: 52.8 us -> 54.7 us
    pallas_call x1, Pallas kernels: 52.8 us -> 54.7 us  [body(): pl.pallas_call(functools.partial(kernel, layout, n_group), out_shape=jax....]
where the time goes in v4:
time: 57.5 us; the launch traced here: 57.4 us
  Pallas kernels  54.7 us (95%)
  other arithmetic  1.98 us (3%)
  between operations  0.67 us (1%)
    pallas_call x1, Pallas kernels, body(): pl.pallas_call(functools.partial(kernel, layout, n_group), out_shape=jax....  54.7 us
    add x1, other arithmetic, body(): return (residual - change[0], coeffs + change[1])  1.98 us

profile of v4, /device:TPU:0, one launch (start us, length us, event | category | flops | bytes accessed | tf_op | source)
XLA Modules:
  0.0 57.4 jit_solution(1461629635092862929)
XLA Ops:
  0.6 0.0 copy-start
  0.6 0.0 copy-start.1
  0.7 54.7 %shard_map.68 = f32[2,147,512]{2,1,0:T(8,128)} custom-call(s32[2]{0:T(128)} %owners_in.1, s32[2]{0:T(128)} %offsets_in.1, f32[440,512]{1,0:T(8,128)} %points_in.1, f32[147,512]{1,0:T(8,128)} %residual_in.1), custom_call_target="tpu_custom_call" | custom-call | tf_op jit(solution)/shard_map/pallas_call | solution.py:456
  55.4 0.0 copy-done
  55.4 0.0 copy-done.1
  55.4 2.0 %bitcast_add_fusion = (f32[147,512]{1,0:T(8,128)}, f32[147,512]{1,0:T(8,128)}) fusion(f32[147,512]{1,0:T(8,128)S(1)} %copy-done.1, f32[2,147,512]{2,1,0:T(8,128)} %shard_map.68, f32[147,512]{1,0:T(8,128)S(1)} %copy-done), kind=kLoop, calls=%fused_computation | loop fusion | flops 150528 | bytes 1806336 | tf_op jit(solution)/shard_map/add | solution.py:478
Async XLA Ops:
  0.6 54.7 %copy-start = (f32[147,512]{1,0:T(8,128)S(1)}, f32[147,512]{1,0:T(8,128)}, u32[]{:S(2)}) copy-start(f32[147,512]{1,0:T(8,128)} %residual_in.1) | copy-start | bytes 903172
  0.6 54.7 %copy-start.1 = (f32[147,512]{1,0:T(8,128)S(1)}, f32[147,512]{1,0:T(8,128)}, u32[]{:S(2)}) copy-start(f32[147,512]{1,0:T(8,128)} %param.7) | copy-start | bytes 903172

commit v5 on v3

--- a/solution.py
+++ b/solution.py
@@ -417,10 +417,10 @@
     inverse.rough()
     inverse.rough()
     inverse.fine()
+    inverse.fine()
     grads[0].gather()
     left1.forward()
     right1.forward()
-    inverse.fine()
     half_tile(2)
     half_tile(3)
     inverse.polish()

time: 55.6 us -> 55.6 us (level)
  no operation moved by 1% of the time
where the time goes in v5:
time: 55.6 us; the launch traced here: 55.4 us
  Pallas kernels  52.8 us (95%)
  other arithmetic  1.98 us (4%)
  between operations  0.67 us (1%)
    pallas_call x1, Pallas kernels, body(): pl.pallas_call(functools.partial(kernel, layout, n_group), out_shape=jax....  52.8 us
    add x1, other arithmetic, body(): return (residual - change[0], coeffs + change[1])  1.98 us

profile of v5, /device:TPU:0, one launch (start us, length us, event | category | flops | bytes accessed | tf_op | source)
XLA Modules:
  0.0 55.4 jit_solution(2414157119791544639)
XLA Ops:
  0.6 0.0 copy-start
  0.6 0.0 copy-start.1
  0.7 52.8 %shard_map.68 = f32[2,147,512]{2,1,0:T(8,128)} custom-call(s32[2]{0:T(128)} %owners_in.1, s32[2]{0:T(128)} %offsets_in.1, f32[440,512]{1,0:T(8,128)} %points_in.1, f32[147,512]{1,0:T(8,128)} %residual_in.1), custom_call_target="tpu_custom_call" | custom-call | tf_op jit(solution)/shard_map/pallas_call | solution.py:465
  53.4 0.0 copy-done
  53.5 0.0 copy-done.1
  53.5 2.0 %bitcast_add_fusion = (f32[147,512]{1,0:T(8,128)}, f32[147,512]{1,0:T(8,128)}) fusion(f32[147,512]{1,0:T(8,128)S(1)} %copy-done.1, f32[2,147,512]{2,1,0:T(8,128)} %shard_map.68, f32[147,512]{1,0:T(8,128)S(1)} %copy-done), kind=kLoop, calls=%fused_computation | loop fusion | flops 150528 | bytes 1806336 | tf_op jit(solution)/shard_map/add | solution.py:486
Async XLA Ops:
  0.6 52.8 %copy-start = (f32[147,512]{1,0:T(8,128)S(1)}, f32[147,512]{1,0:T(8,128)}, u32[]{:S(2)}) copy-start(f32[147,512]{1,0:T(8,128)} %residual_in.1) | copy-start | bytes 903172
  0.6 52.8 %copy-start.1 = (f32[147,512]{1,0:T(8,128)S(1)}, f32[147,512]{1,0:T(8,128)}, u32[]{:S(2)}) copy-start(f32[147,512]{1,0:T(8,128)} %param.7) | copy-start | bytes 903172
